TPU v7x, 256 devices: a whole 4x4x8 slice. The times are simulated.
256 devices in a mesh: ha: 16 (over z_hi, y), wa: 8 (over x, core), col: 2 (over z_lo).
Axes of the slice: x: 4, y: 4, z: 8 (z_hi: 4, z_lo: 2; z = z_hi * 2 + z_lo), core: 2. Of those that a mesh axis runs over, the one named last changes fastest.
Arguments:
- features: bfloat16 [2, 4, 64, 256, 96], P('col', None, 'ha', 'wa'), may hold values from -6 to 6
- gain_first: float32 [96], replicated, may hold values from 0.1 to 1.9
- bias_first: float32 [96], replicated, may hold values from -3 to 3
- kernel_first: bfloat16 [3, 3, 3, 96, 96], replicated, may hold values from -0.125 to 0.125
- gain_second: float32 [96], replicated, may hold values from 0.1 to 1.9
- bias_second: float32 [96], replicated, may hold values from -3 to 3
- kernel_second: bfloat16 [3, 3, 3, 96, 96], replicated, may hold values from -0.125 to 0.125
- reward_map: bfloat16 [2, 4, 64, 256, 96], P('col', None, 'ha', 'wa'), may hold values from -6 to 6
- target_scores: float32 [2], replicated, may hold values from -5 to 5
Outputs:
- grad_input: float32 [2, 4, 64, 256, 96], P('col', None, 'ha', 'wa')
- weight_grad: float32 [2, 3, 3, 3, 96, 96], P(None, None, None, None, 'ha')
All inputs are finite; a program needn't handle non-finite values.
Results may differ from a plain program's by a relative error of at most 0.0049.
Values may be sent and summed in bfloat16 or wider, within the bound.
No kernel may reach another device: no remote copies, remote signals or barrier semaphores. Data moves between devices by JAX's collectives and lax.ppermute only.
A program may use at most 64 MiB of HBM per device.

v0:
```python
import jax
import jax.numpy as jnp
from jax import lax
from jax.sharding import PartitionSpec as P


def extended(cells, sides, width):
    for axis, dim in sides:
        count = lax.axis_size(axis)
        ends = count - 1
        head = lax.slice_in_dim(cells, 0, width, axis=dim)
        tail = lax.slice_in_dim(cells, cells.shape[dim] - width, cells.shape[dim], axis=dim)
        cells = jnp.concatenate(
            [
                lax.ppermute(tail, axis, [(i, (i + 1) % count) for i in range(ends)]),
                cells,
                lax.ppermute(head, axis, [((i + 1) % count, i) for i in range(ends)]),
            ],
            axis=dim,
        )
    return cells


def activate(values, gain):
    scaled = lax.rsqrt(jnp.mean(values * values, axis=-1, keepdims=True) + 1e-06)
    return jax.nn.silu(values * scaled * gain)


def activate_back(values, gain, cotangent):
    _, pull = jax.vjp(lambda inner: activate(inner, gain), values)
    return pull(cotangent)[0]


def conv_forward(padded, kernel):
    frames, height, across, channels = padded.shape
    out_h = height - 2
    out_w = across - 2
    timed = jnp.concatenate([jnp.zeros((2, height, across, channels), padded.dtype), padded], 0)
    summed = jnp.zeros((frames * out_h * out_w, kernel.shape[-1]), jnp.float32)
    for step_t in range(3):
        for step_h in range(3):
            for step_w in range(3):
                window = timed[
                    step_t : step_t + frames, step_h : step_h + out_h, step_w : step_w + out_w
                ].reshape(-1, channels)
                summed = summed + jnp.dot(
                    window, kernel[step_t, step_h, step_w], preferred_element_type=jnp.float32
                )
    return summed.reshape(frames, out_h, out_w, -1)


def conv_transpose(padded, kernel):
    frames, height, across, channels = padded.shape
    out_h = height - 2
    out_w = across - 2
    timed = jnp.concatenate([padded, jnp.zeros((2, height, across, channels), padded.dtype)], 0)
    summed = jnp.zeros((frames * out_h * out_w, kernel.shape[3]), jnp.float32)
    for step_t in range(3):
        for step_h in range(3):
            for step_w in range(3):
                window = timed[
                    2 - step_t : 2 - step_t + frames,
                    2 - step_h : 2 - step_h + out_h,
                    2 - step_w : 2 - step_w + out_w,
                ].reshape(-1, channels)
                summed = summed + lax.dot_general(
                    window,
                    kernel[step_t, step_h, step_w],
                    (((1,), (1,)), ((), ())),
                    preferred_element_type=jnp.float32,
                )
    return summed.reshape(frames, out_h, out_w, -1)


def kernel_grad(padded, grad_out):
    frames, height, across, channels = padded.shape
    out_h = height - 2
    out_w = across - 2
    timed = jnp.concatenate([jnp.zeros((2, height, across, channels), padded.dtype), padded], 0)
    flat_out = grad_out.reshape(-1, grad_out.shape[-1])
    pieces = []
    for step_t in range(3):
        for step_h in range(3):
            for step_w in range(3):
                window = timed[
                    step_t : step_t + frames, step_h : step_h + out_h, step_w : step_w + out_w
                ].reshape(-1, channels)
                pieces.append(
                    lax.dot_general(
                        window,
                        flat_out,
                        (((0,), (0,)), ((), ())),
                        preferred_element_type=jnp.float32,
                    )
                )
    return jnp.stack(pieces).reshape(3, 3, 3, channels, flat_out.shape[-1])


def local(
    features,
    gain_first,
    bias_first,
    kernel_first,
    gain_second,
    bias_second,
    kernel_second,
    reward_map,
    target_scores,
):
    local_x = features[0]
    local_g = reward_map[0]
    frames, height, across, channels = local_x.shape
    feats = local_x.astype(jnp.float32)
    norm_reward = jnp.sqrt(
        jnp.float32(frames * height * lax.axis_size("ha") * across * lax.axis_size("wa") * channels)
    )
    first = activate(feats, gain_first).astype(jnp.bfloat16)
    first_pad = extended(first, (("ha", 1), ("wa", 2)), 1)
    hidden = conv_forward(first_pad, kernel_first) + bias_first
    second = activate(hidden, gain_second).astype(jnp.bfloat16)
    second_pad = extended(second, (("ha", 1), ("wa", 2)), 1)
    output = feats + conv_forward(second_pad, kernel_second) + bias_second
    partial_value = jnp.sum(output * local_g.astype(jnp.float32)) / norm_reward
    mine = lax.axis_index("col")
    whole = lax.psum(partial_value, ("ha", "wa"))
    rewards = lax.all_gather(whole.reshape(1), "col", axis=0, tiled=True)
    prob = 1.0 / (1.0 + jnp.exp(rewards[1 - mine] - rewards[mine]))
    target = 1.0 / (1.0 + jnp.exp(target_scores[1 - mine] - target_scores[mine]))
    delta = prob - target
    cot = delta * local_g.astype(jnp.float32)
    cot_low = cot.astype(jnp.bfloat16)
    cot_pad = extended(cot_low, (("ha", 1), ("wa", 2)), 1)
    back_second = conv_transpose(cot_pad, kernel_second)
    grad_hidden = activate_back(hidden, gain_second, back_second).astype(jnp.bfloat16)
    grad_pad = extended(grad_hidden, (("ha", 1), ("wa", 2)), 1)
    grad_two = kernel_grad(second_pad, cot_low)
    back_first = conv_transpose(grad_pad, kernel_first)
    grad_one = kernel_grad(first_pad, grad_hidden)
    grad_local = cot + activate_back(feats, gain_first, back_first)
    share = channels // lax.axis_size("ha")
    summed_one, summed_two = lax.psum((grad_one, grad_two), ("ha", "wa", "col"))
    start = lax.axis_index("ha") * share
    summed_one = lax.dynamic_slice_in_dim(summed_one, start, share, 3)
    summed_two = lax.dynamic_slice_in_dim(summed_two, start, share, 3)
    scale_weight = 1.0 / jnp.sqrt(
        jnp.float32(frames * height * lax.axis_size("ha") * across * lax.axis_size("wa"))
    )
    weights_out = jnp.stack([summed_one, summed_two]) * scale_weight
    return (grad_local[None], weights_out)


def solution(mesh):
    placed = (
        P("col", None, "ha", "wa", None),
        P(),
        P(),
        P(),
        P(),
        P(),
        P(),
        P("col", None, "ha", "wa", None),
        P(),
    )
    return jax.shard_map(
        local,
        mesh=mesh,
        in_specs=placed,
        out_specs=(P("col", None, "ha", "wa", None), P(None, None, None, None, "ha", None)),
        check_vma=False,
    )
```

profile of v0, /device:TPU:1, one launch (start us, length us, event | category | flops | bytes accessed | tf_op | source)
XLA Modules:
  0.0 761.4 jit_solution(2760302660211814418)
XLA Ops:
  7.2 1.1 fusion.127
  8.3 1.1 fusion.135
  9.4 4.0 collective-permute-start
  13.4 1.3 collective-permute-start.1
  14.7 1.1 fusion.126
  15.8 1.7 copy.23
  17.6 1.7 copy.24
  21.9 4.0 collective-permute-start.2
  25.8 1.9 collective-permute-start.3
  27.8 3.0 collective-permute-done.3
  39.4 4.3 collective-permute-start.4
  43.7 1.3 collective-permute-start.5
  45.4 3.0 collective-permute-done.5
  48.4 3.4 collective-permute-start.6
  51.8 1.9 collective-permute-start.7
  53.8 3.0 collective-permute-done.7
  63.4 0.9 fusion.87
  64.9 343.6 %psum.21 = f32[1]{0:T(128)} all-reduce(f32[1]{0:T(128)} %bitcast.111), channel_id=1, replica_groups=mesh['ha'=16,'wa'=8,'col'=2] {'ha','wa'}, use_global_device_ids=true, to_apply=%region_3.4 | all-reduce | flops 1 | bytes 8 | tf_op jit(solution)/shard_map/psum | solution.py:125
  409.0 2.5 dynamic-update-slice
  412.3 3.9 all-reduce.4
  418.3 1.3 collective-permute-start.8
  419.6 1.3 collective-permute-start.9
  427.1 2.5 collective-permute-start.10
  429.6 8.4 %collective-permute-start.11 = (bf16[4,6,1,96]{3,2,1,0:T(2,128)(2,1)S(1)}, bf16[4,6,1,96]{3,2,1,0:T(2,128)(2,1)S(1)}, u32[]{:S(2)}, u32[]{:S(2)}) collective-permute-start(bf16[4,6,1,96]{3,2,1,0:T(2,128)(2,1)S(1)} %get-tuple-element.108), channel_id=1, source_target_pairs={{2,0},{4,2},{6,4},{8,6},{10,8},{12,10},{14,12},{3,1},{5,3},{7,5},{... | collective-permute-start | bytes 13832 | tf_op jit(solution)/shard_map/ppermute | solution.py:17
  445.2 0.8 fusion.66
  446.5 0.8 fusion.65
  447.4 0.8 fusion.64
  454.1 0.9 fusion.56
  454.9 0.9 fusion.55
  455.8 0.8 fusion.54
  456.6 0.8 fusion.53
  457.5 0.8 fusion.52
  459.1 0.8 fusion.50
  460.0 0.8 fusion.49
  461.7 0.8 fusion.16
  465.0 0.8 fusion.44
  465.8 0.8 fusion.43
  466.7 4.3 collective-permute-start.12
  470.9 1.3 collective-permute-start.13
  472.2 0.8 fusion.15
  473.9 1.7 collective-permute-done.13
  475.6 1.9 collective-permute-start.14
  477.6 3.1 collective-permute-start.15
  480.7 1.9 collective-permute-done.15
  488.8 1.0 fusion.118
  489.7 262.1 %all-reduce.8.cloned.1.call-done = (f32[3,3,3,96,96]{4,3,2,1,0:T(8,128)}, f32[3,3,3,96,96]{4,3,2,1,0:T(8,128)}) async-done(((f32[3,3,3,96,96]{4,3,2,1,0:T(8,128)}, f32[3,3,3,96,96]{4,3,2,1,0:T(8,128)}), (f32[3,3,3,96,96]{4,3,2,1,0:T(8,128)}, f32[3,3,3,96,96]{4,3,2,1,0:T(8,128)})) %all-reduce.8.cloned.1.call-update) | async-done | bytes 1990672 | tf_op jit(solution)/shard_map/psum | solution.py:141
  751.8 1.0 dynamic-slice_bitcast_fusion.1
  752.8 1.0 dynamic-slice_bitcast_fusion
  (289 shorter events, 49.4 us)
Async XLA Ops:
  7.2 14.1 %copy-start.35 = (u32[256]{0:T(256)S(1)}, u32[256]{0:T(256)}, u32[]{:S(2)}) copy-start(u32[256]{0:T(256)} %constant.65) | copy-start | bytes 3076
  7.2 12.1 %copy-start.33 = (f32[2]{0:T(128)S(1)}, f32[2]{0:T(128)}, u32[]{:S(2)}) copy-start(f32[2]{0:T(128)} %param.17) | copy-start | bytes 28
  7.2 744.6 %all-reduce.8.cloned.1.call-start = ((), (), s32[]{:S(2)}) async-start(), calls=%async_computation | async-start | bytes 5308416 | tf_op jit(solution)/shard_map/psum | solution.py:141
  8.3 22.6 %copy-start.20 = (f32[4,4,32]{2,1,0:T(4,128)}, f32[4,4,32]{2,1,0:T(4,128)S(1)}, u32[]{:S(2)}) copy-start(f32[4,4,32]{2,1,0:T(4,128)S(1)} %fusion.127) | copy-start | bytes 6148
  9.4 12.4 %collective-permute-start = (bf16[4,1,32,96]{3,2,1,0:T(8,128)(2,1)S(1)}, bf16[4,1,32,96]{3,2,1,0:T(8,128)(2,1)S(1)}, u32[]{:S(2)}, u32[]{:S(2)}) collective-permute-start(bf16[4,1,32,96]{3,2,1,0:T(8,128)(2,1)S(1)} %get-tuple-element.132), channel_id=1, source_target_pairs={{0,16},{16,32},{32,48},{48,64},{64,80},{80,96},{96,112},{112,128},... | collective-permute-start | bytes 73736 | tf_op jit(solution)/shard_map/ppermute | solution.py:15
  13.4 8.4 %collective-permute-start.1 = (bf16[4,1,32,96]{3,2,1,0:T(8,128)(2,1)S(1)}, bf16[4,1,32,96]{3,2,1,0:T(8,128)(2,1)S(1)}, u32[]{:S(2)}, u32[]{:S(2)}) collective-permute-start(bf16[4,1,32,96]{3,2,1,0:T(8,128)(2,1)S(1)} %get-tuple-element.133), channel_id=1, source_target_pairs={{16,0},{32,16},{48,32},{64,48},{80,64},{96,80},{112,96},{128,112},... | collective-permute-start | bytes 73736 | tf_op jit(solution)/shard_map/ppermute | solution.py:17
  15.8 21.7 %copy-start.17 = (bf16[1,4,4,32,96]{4,3,2,1,0:T(8,128)(2,1)}, bf16[1,4,4,32,96]{4,3,2,1,0:T(8,128)(2,1)S(1)}, u32[]{:S(2)}) copy-start(bf16[1,4,4,32,96]{4,3,2,1,0:T(8,128)(2,1)S(1)} %fusion.126) | copy-start | bytes 294916
  21.8 10.5 %copy-start.11 = (bf16[4,1,32,96]{3,2,1,0:T(8,128)(2,1)}, bf16[4,1,32,96]{3,2,1,0:T(8,128)(2,1)S(1)}, u32[]{:S(2)}) copy-start(bf16[4,1,32,96]{3,2,1,0:T(8,128)(2,1)S(1)} %collective-permute-done) | copy-start | bytes 73732
  21.9 6.0 collective-permute-start.2
  25.8 5.0 collective-permute-start.3
  31.0 1.1 copy-start.1
  37.1 1.2 copy-start.28
  37.6 1.6 copy-start.31
  38.0 7.1 copy-start.2
  39.1 18.2 %copy-start.24 = (f32[512]{0:T(512)}, f32[512]{0:T(512)S(1)}, u32[]{:S(2)}) copy-start(f32[512]{0:T(512)S(1)} %get-tuple-element.134) | copy-start | bytes 6148
  39.2 4.5 copy-start.22
  39.4 6.0 collective-permute-start.4
  43.7 4.7 collective-permute-start.5
  45.4 12.2 %copy-start.15 = (bf16[4,1,32,96]{3,2,1,0:T(8,128)(2,1)}, bf16[4,1,32,96]{3,2,1,0:T(8,128)(2,1)S(1)}, u32[]{:S(2)}) copy-start(bf16[4,1,32,96]{3,2,1,0:T(8,128)(2,1)S(1)} %collective-permute-done.4) | copy-start | bytes 73732
  48.3 9.2 %copy-start.13 = (bf16[4,1,32,96]{3,2,1,0:T(8,128)(2,1)}, bf16[4,1,32,96]{3,2,1,0:T(8,128)(2,1)S(1)}, u32[]{:S(2)}) copy-start(bf16[4,1,32,96]{3,2,1,0:T(8,128)(2,1)S(1)} %collective-permute-done.5) | copy-start | bytes 73732
  48.4 5.4 collective-permute-start.6
  51.8 5.0 collective-permute-start.7
  62.4 0.9 copy-start.9
  62.4 1.0 copy-start.10
  62.4 1.0 copy-start.34
  62.9 355.3 %copy-start.3 = (bf16[1,4,4,32,96]{4,3,2,1,0:T(8,128)(2,1)S(1)}, bf16[1,4,4,32,96]{4,3,2,1,0:T(8,128)(2,1)}, u32[]{:S(2)}) copy-start(bf16[1,4,4,32,96]{4,3,2,1,0:T(8,128)(2,1)} %param.16) | copy-start | bytes 294916
  418.3 8.8 %collective-permute-start.8 = (bf16[4,1,32,96]{3,2,1,0:T(8,128)(2,1)S(1)}, bf16[4,1,32,96]{3,2,1,0:T(8,128)(2,1)S(1)}, u32[]{:S(2)}, u32[]{:S(2)}) collective-permute-start(bf16[4,1,32,96]{3,2,1,0:T(8,128)(2,1)S(1)} %get-tuple-element.124), channel_id=1, source_target_pairs={{0,16},{16,32},{32,48},{48,64},{64,80},{80,96},{96,112},{112,128},... | collective-permute-start | bytes 73736 | tf_op jit(solution)/shard_map/ppermute | solution.py:15
  419.6 7.5 collective-permute-start.9
  423.8 1.4 copy-start.16
  424.5 1.4 copy-start.19
  425.2 1.4 copy-start.14
  427.0 11.1 %copy-start.8 = (f32[27,96,96]{2,1,0:T(8,128)}, f32[27,96,96]{2,1,0:T(8,128)S(1)}, u32[]{:S(2)}) copy-start(f32[27,96,96]{2,1,0:T(8,128)S(1)} %fusion.17) | copy-start | bytes 2985988
  427.1 11.0 %collective-permute-start.10 = (bf16[4,6,1,96]{3,2,1,0:T(2,128)(2,1)S(1)}, bf16[4,6,1,96]{3,2,1,0:T(2,128)(2,1)S(1)}, u32[]{:S(2)}, u32[]{:S(2)}) collective-permute-start(bf16[4,6,1,96]{3,2,1,0:T(2,128)(2,1)S(1)} %get-tuple-element.109), channel_id=1, source_target_pairs={{0,2},{2,4},{4,6},{6,8},{8,10},{10,12},{12,14},{1,3},{3,5},{5,7},{... | collective-permute-start | bytes 13832 | tf_op jit(solution)/shard_map/ppermute | solution.py:15
  429.6 9.1 %collective-permute-start.11 = (bf16[4,6,1,96]{3,2,1,0:T(2,128)(2,1)S(1)}, bf16[4,6,1,96]{3,2,1,0:T(2,128)(2,1)S(1)}, u32[]{:S(2)}, u32[]{:S(2)}) collective-permute-start(bf16[4,6,1,96]{3,2,1,0:T(2,128)(2,1)S(1)} %get-tuple-element.108), channel_id=1, source_target_pairs={{2,0},{4,2},{6,4},{8,6},{10,8},{12,10},{14,12},{3,1},{5,3},{7,5},{... | collective-permute-start | bytes 13832 | tf_op jit(solution)/shard_map/ppermute | solution.py:17
  443.4 1.0 copy-start.25
  443.4 1.0 copy-start.29
  443.4 1.0 copy-start.32
  455.8 5.0 copy-start.7
  456.6 5.0 copy-start.12
  457.5 5.0 copy-start.5
  459.1 5.0 copy-start.18
  466.7 7.3 collective-permute-start.12
  470.9 4.7 collective-permute-start.13
  475.6 5.0 collective-permute-start.14
  477.6 5.0 collective-permute-start.15
  487.5 0.9 copy-start
  487.5 0.9 copy-start.30
  487.7 1.1 copy-start.21
  (5 other events, 3.7 us)
Sparse Core Ops, SparseCore 0:
  474.1 277.7 all-reduce.7
where the time goes:
time: 764 us; the launch traced here: 761 us
  blocking collectives  347 us (45%)
  waiting for transfers between devices  275 us (36%)
  matrix products  50.9 us (7%)
  starting transfers between devices  46.1 us (6%)
  between operations  19.1 us (3%)
  local copies, waits for them, and re-layouts  15.8 us (2%)
    psum x1, blocking collectives, local(): whole = lax.psum(partial_value, ('ha', 'wa'))  344 us
    psum x1, waiting for transfers between devices, local(): summed_one, summed_two = lax.psum((grad_one, grad_two), ('ha', 'wa', 'col'))  262 us
    dot_general x54, matrix products, kernel_grad(): lax.dot_general(window, flat_out, (((0,), (0,)), ((), ())), preferred_ele...  28.6 us
    ppermute x8, starting transfers between devices, extended(): lax.ppermute(tail, axis, [(i, (i + 1) % count) for i in range(ends)])  25.6 us
    ppermute x8, starting transfers between devices, extended(): lax.ppermute(head, axis, [((i + 1) % count, i) for i in range(ends)])  20.5 us
  transfers between devices with their start and end apart: 17, of which 7 were waited for; matrix products, arithmetic and copies ran while one was open for 3% of the time, Pallas kernels for 0%

commit v1 on v0

v1 whole, which is shorter than its diff:
```python
import jax
import jax.numpy as jnp
from jax import lax
from jax.experimental import pallas as pl
from jax.experimental.pallas import tpu as pltpu
from jax.sharding import PartitionSpec as P

F32 = jnp.float32
BF16 = jnp.bfloat16
EPS = 1e-06
LANES = 128
PITCH = 48


def dot(a, b, dims):
    return lax.dot_general(a, b, (dims, ((), ())), preferred_element_type=F32)


def act_parts(values, gain, channels):
    scale = lax.rsqrt(jnp.sum(values * values, axis=-1, keepdims=True) * (1.0 / channels) + EPS)
    inner = values * scale * gain
    sig = 1.0 / (1.0 + jnp.exp(-inner))
    return scale, inner, sig


def act_back(values, parts, gain, cotangent, channels):
    scale, inner, sig = parts
    pulled = cotangent * (sig * (1.0 + inner * (1.0 - sig))) * gain
    along = jnp.sum(pulled * values, axis=-1, keepdims=True) * (1.0 / channels)
    return scale * pulled - values * (scale * scale * scale * along)


def block_kernel(
    edge,
    ext,
    feats_own,
    map_own,
    k_first,
    k_second,
    vectors,
    perm,
    grad,
    packed,
    wide,
    first3,
    map3,
    hid,
    back3,
    w1f,
    w1b,
    w2b,
    taps,
):
    channels = feats_own.shape[-1]
    frames, rows, across = feats_own.shape[:3]
    gain_first = vectors[0:1]
    bias_first = vectors[1:2]
    gain_second = vectors[2:3]
    bias_second = vectors[3:4]

    w1f[...] = jnp.zeros_like(w1f)
    w1b[...] = jnp.zeros_like(w1b)
    w2b[...] = jnp.zeros_like(w2b)
    for tap in range(27):
        pair, dj = divmod(tap, 3)
        one = k_first[tap]
        w1f[pair, LANES * dj : LANES * dj + channels, 0:channels] = one
        w1b[pair, 0:channels, LANES * (2 - dj) : LANES * (2 - dj) + channels] = one
        w2b[pair, 0:channels, LANES * (2 - dj) : LANES * (2 - dj) + channels] = k_second[tap]

    wide[...] = jnp.zeros_like(wide)
    halo_w = ext.shape[2]
    wide[:, :, 0:halo_w, 0:channels] = ext[0:frames].astype(F32)
    feats = wide[...]
    _, inner, sig = act_parts(feats, gain_first, channels)
    wide[...] = inner * sig
    first3[0:2] = jnp.zeros((2,) + first3.shape[1:], BF16)
    for dj in range(3):
        first3[2:6, :, :, LANES * dj : LANES * (dj + 1)] = wide[:, :, dj : dj + PITCH, :].astype(BF16)
    wide[:, :, 0:halo_w, 0:channels] = ext[frames : 2 * frames].astype(F32)
    map3[4:6] = jnp.zeros((2,) + map3.shape[1:], BF16)
    for dj in range(3):
        map3[0:4, :, :, LANES * dj : LANES * (dj + 1)] = wide[:, :, dj : dj + PITCH, :].astype(BF16)

    count = frames * (rows + 2) * PITCH
    hidden = jnp.zeros((count, LANES), F32)
    back = jnp.zeros((count, LANES), F32)
    for pair in range(9):
        dt, di = divmod(pair, 3)
        hidden = hidden + dot(
            first3[dt : dt + frames, di : di + rows + 2].reshape(count, 3 * LANES), w1f[pair], ((1,), (0,))
        )
    hidden = hidden + bias_first
    for pair in range(9):
        dt, di = divmod(pair, 3)
        back = back + dot(
            map3[2 - dt : 2 - dt + frames, 2 - di : 4 - di + rows].reshape(count, 3 * LANES),
            w2b[pair],
            ((1,), (1,)),
        )

    parts = act_parts(hidden, gain_second, channels)
    shape4 = (frames, rows + 2, PITCH, LANES)
    row = lax.broadcasted_iota(jnp.int32, shape4, 1)
    column = lax.broadcasted_iota(jnp.int32, shape4, 2)
    own = (column >= 1) & (column <= across)
    second = jnp.where(own, (parts[1] * parts[2]).reshape(shape4), 0.0)[:, 1 : rows + 1].astype(BF16)
    back4 = back.reshape(shape4)[:, 1 : rows + 1]
    own_f = feats_own[...].astype(F32)
    own_g = map_own[...].astype(F32)
    value = jnp.sum(second.astype(F32) * back4) + jnp.sum(own_g * (own_f + bias_second[:, 0:channels]))

    inside = (
        (row >= edge[0])
        & (row <= edge[1])
        & (column >= edge[2])
        & (column <= edge[3])
    )
    pulled = act_back(hidden, parts, gain_second, back, channels).reshape(shape4)
    hid[...] = jnp.where(inside, pulled, 0.0)
    back3[4:6] = jnp.zeros((2,) + back3.shape[1:], BF16)
    for dj in range(3):
        back3[0:4, :, :, LANES * dj : LANES * (dj + 1)] = hid[:, :, dj : dj + across, :].astype(BF16)

    def pack(which):
        lane = lax.broadcasted_iota(jnp.int32, (channels, LANES), 1)
        for group in range(7):
            if group == 6:
                last = jnp.full((channels, LANES), value, F32)
            else:
                last = taps[4 * group + 3]
            for k in range(3):
                tile = jnp.where(lane < channels, taps[4 * group + k], pltpu.roll(last, 96 - 32 * k, 1))
                for y in range(4):
                    for z in range(4):
                        packed[which, y, 42 * z + 6 * group : 42 * z + 6 * group + 6, LANES * k : LANES * (k + 1)] = tile[
                            24 * y + 6 * z : 24 * y + 6 * z + 6
                        ]

    turned = dot(perm[...], second.reshape(-1, LANES), ((1,), (1,))).astype(BF16)
    for pair in range(9):
        dt, di = divmod(pair, 3)
        got = dot(
            turned,
            map3[2 - dt : 2 - dt + frames, 3 - di : 3 - di + rows].reshape(-1, 3 * LANES),
            ((1,), (0,)),
        )
        for dj in range(3):
            taps[3 * pair + dj] = got[:, LANES * (2 - dj) : LANES * (3 - dj)]
    pack(1)

    first_own = first3[2 : 2 + frames, 2 : 2 + rows, 0:across, 2 * LANES : 3 * LANES].reshape(-1, LANES)
    turned = dot(perm[...], first_own, ((1,), (1,))).astype(BF16)
    low = jnp.zeros((frames * rows * across, LANES), F32)
    for pair in range(9):
        dt, di = divmod(pair, 3)
        moved = back3[2 - dt : 2 - dt + frames, 2 - di : 2 - di + rows].reshape(-1, 3 * LANES)
        low = low + dot(moved, w1b[pair], ((1,), (1,)))
        got = dot(turned, moved, ((1,), (0,)))
        for dj in range(3):
            taps[3 * pair + dj] = got[:, LANES * (2 - dj) : LANES * (3 - dj)]
    pack(0)

    gain_own = gain_first[:, 0:channels]
    parts = act_parts(own_f, gain_own, channels)
    low4 = low.reshape(frames, rows, across, LANES)[..., 0:channels]
    grad[...] = own_g + act_back(own_f, parts, gain_own, low4, channels)


def local_block(edge, ext, feats_own, map_own, k_first, k_second, vectors, perm):
    frames, rows, across, channels = feats_own.shape
    vmem = pl.BlockSpec(memory_space=pltpu.VMEM)
    return pl.pallas_call(
        block_kernel,
        out_shape=(
            jax.ShapeDtypeStruct(feats_own.shape, F32),
            jax.ShapeDtypeStruct((2, 4, 168, 3 * LANES), F32),
        ),
        in_specs=[pl.BlockSpec(memory_space=pltpu.SMEM)] + [vmem] * 7,
        out_specs=(vmem, vmem),
        scratch_shapes=[
            pltpu.VMEM((frames, rows + 4, PITCH + 8, LANES), F32),
            pltpu.VMEM((frames + 2, rows + 4, PITCH, 3 * LANES), BF16),
            pltpu.VMEM((frames + 2, rows + 4, PITCH, 3 * LANES), BF16),
            pltpu.VMEM((frames, rows + 2, PITCH, LANES), F32),
            pltpu.VMEM((frames + 2, rows + 2, across, 3 * LANES), BF16),
            pltpu.VMEM((9, 3 * LANES, LANES), BF16),
            pltpu.VMEM((9, LANES, 3 * LANES), BF16),
            pltpu.VMEM((9, LANES, 3 * LANES), BF16),
            pltpu.VMEM((27, channels, LANES), F32),
        ],
        compiler_params=pltpu.CompilerParams(vmem_limit_bytes=48 * 1024 * 1024),
        cost_estimate=pl.CostEstimate(flops=3_000_000_000, bytes_accessed=6_000_000, transcendentals=500_000),
    )(edge, ext, feats_own, map_own, k_first, k_second, vectors, perm)


def extended(cells, axis, dim, width):
    count = lax.axis_size(axis)
    ends = count - 1
    head = lax.slice_in_dim(cells, 0, width, axis=dim)
    tail = lax.slice_in_dim(cells, cells.shape[dim] - width, cells.shape[dim], axis=dim)
    return jnp.concatenate(
        [
            lax.ppermute(tail, axis, [(i, (i + 1) % count) for i in range(ends)]),
            cells,
            lax.ppermute(head, axis, [((i + 1) % count, i) for i in range(ends)]),
        ],
        axis=dim,
    )


def swap(values, axis, flip):
    return lax.ppermute(values, axis, [(i, i ^ flip) for i in range(lax.axis_size(axis))])


def pick(values, index):
    return lax.dynamic_index_in_dim(values, index, 0, keepdims=False)


def local(
    features,
    gain_first,
    bias_first,
    kernel_first,
    gain_second,
    bias_second,
    kernel_second,
    reward_map,
    target_scores,
):
    frames, rows, across, channels = features.shape[1:]
    count_h = lax.axis_size("ha")
    count_w = lax.axis_size("wa")
    at_h = lax.axis_index("ha")
    at_w = lax.axis_index("wa")
    at_col = lax.axis_index("col")
    core = at_w % 2
    at_y = at_h % 4
    at_z = at_h // 4

    both = jnp.concatenate([features[0], reward_map[0]], 0)
    ext = extended(extended(both, "ha", 1, 2), "wa", 2, 2)
    edge = jnp.stack(
        [
            jnp.where(at_h == 0, 1, 0),
            jnp.where(at_h == count_h - 1, rows, rows + 1),
            jnp.where(at_w == 0, 1, 0),
            jnp.where(at_w == count_w - 1, across, across + 1),
        ]
    ).astype(jnp.int32)
    vectors = jnp.pad(
        jnp.stack([gain_first, bias_first, gain_second, bias_second]), ((0, 4), (0, LANES - channels))
    )
    place = lax.broadcasted_iota(jnp.int32, (channels, LANES), 0)
    source = 24 * ((place // 6) % 4) + 6 * (place // 24) + place % 6
    perm = (lax.broadcasted_iota(jnp.int32, (channels, LANES), 1) == source).astype(BF16)
    grad, packed = local_block(
        edge,
        ext,
        features[0],
        reward_map[0],
        kernel_first.reshape(27, channels, channels),
        kernel_second.reshape(27, channels, channels),
        vectors,
        perm,
    )

    held = pick(packed, core) + swap(pick(packed, 1 - core), "wa", 1)
    got = [swap(pick(held, at_y ^ k), "ha", k) for k in (1, 2, 3)]
    held = (pick(held, at_y) + got[0]) + (got[1] + got[2])
    held = held.reshape(4, 42, 3 * LANES)
    got = [swap(pick(held, at_z ^ k), "ha", 4 * k) for k in (1, 2, 3)]
    held = (pick(held, at_z) + got[0]) + (got[1] + got[2])
    got = [swap(held, "wa", 2 * k) for k in (1, 2, 3)]
    held = (held + got[0]) + (got[1] + got[2])
    other = swap(held, "col", 1)
    each = [jnp.where(at_col == 0, held, other), jnp.where(at_col == 0, other, held)]
    total = count_h * count_w * rows * across * frames
    norm_reward = jnp.sqrt(jnp.float32(total * channels))
    rewards = [part[36, 96] / norm_reward for part in each]
    deltas = []
    for n in range(2):
        prob = 1.0 / (1.0 + jnp.exp(rewards[1 - n] - rewards[n]))
        target = 1.0 / (1.0 + jnp.exp(target_scores[1 - n] - target_scores[n]))
        deltas.append(prob - target)
    summed = (each[0] * deltas[0] + each[1] * deltas[1]) * (1.0 / jnp.sqrt(jnp.float32(total)))
    mate = swap(summed, "wa", 1)
    pair = jnp.stack([jnp.where(core == 0, summed, mate), jnp.where(core == 0, mate, summed)])
    pair = pair.reshape(2, 7, 6, 3, LANES)
    main = jnp.moveaxis(pair[..., 0:channels], 3, 2)
    rest = pair[..., channels:LANES].reshape(2, 7, 6, 1, channels)
    rest = jnp.moveaxis(rest, 3, 2)
    weights = jnp.concatenate([main, rest], axis=2).reshape(2, 28, 6, channels)[:, 0:27]
    mine = jnp.where(at_col == 0, deltas[0], deltas[1])
    return ((grad * mine)[None], weights.reshape(2, 3, 3, 3, 6, channels))


def solution(mesh):
    placed = (
        P("col", None, "ha", "wa", None),
        P(),
        P(),
        P(),
        P(),
        P(),
        P(),
        P("col", None, "ha", "wa", None),
        P(),
    )
    return jax.shard_map(
        local,
        mesh=mesh,
        in_specs=placed,
        out_specs=(P("col", None, "ha", "wa", None), P(None, None, None, None, "ha", None)),
        check_vma=False,
    )
```

time: 764 us -> 97.8 us (0.13)
  blocking collectives: 347 us -> 0 us
  waiting for transfers between devices: 275 us -> 28.5 us
  matrix products: 50.9 us -> 0 us
  between operations: 19.1 us -> 5.18 us
  local copies, waits for them, and re-layouts: 15.8 us -> 6.18 us
  Pallas kernels: 0 us -> 8.71 us
    psum x1 -> x0, blocking collectives: 344 us -> none  [local(): whole = lax.psum(partial_value, ('ha', 'wa'))]
    psum x1 -> x0, waiting for transfers between devices: 262 us -> none  [local(): summed_one, summed_two = lax.psum((grad_one, grad_two), ('ha', 'wa', 'col'))]
    dot_general x162 -> x0, matrix products: 50.9 us -> none  [the longest x54 28.6 us: kernel_grad(): lax.dot_general(window, flat_out, (((0,), (0,)), ((), ())), preferred_ele...]
    ppermute x0 -> x12, starting transfers between devices: none -> 28.7 us  [swap(): lax.ppermute(values, axis, [(i, i ^ flip) for i in range(lax.axis_size(ax...]
    ppermute x0 -> x12, waiting for transfers between devices: none -> 26.5 us  [swap(): lax.ppermute(values, axis, [(i, i ^ flip) for i in range(lax.axis_size(ax...]
    ppermute x8 -> x2, starting transfers between devices: 25.6 us -> 6.59 us  [extended(): lax.ppermute(tail, axis, [(i, (i + 1) % count) for i in range(ends)])]
    ppermute x8 -> x2, starting transfers between devices: 20.5 us -> 6.9 us  [extended(): lax.ppermute(head, axis, [((i + 1) % count, i) for i in range(ends)])]
    ppermute x8 -> x2, waiting for transfers between devices: 13.1 us -> 0.01 us  [extended(): lax.ppermute(head, axis, [((i + 1) % count, i) for i in range(ends)])]
  transfers between devices with their start and end apart: 17 -> 16, of which waited for: 7 -> 11; matrix products, arithmetic and copies ran while one was open for 3% -> 2% of each run, Pallas kernels for 0% -> 0%
where the time goes in v1:
time: 97.8 us; the launch traced here: 97.3 us
  starting transfers between devices  42.2 us (43%)
  waiting for transfers between devices  28.5 us (29%)
  Pallas kernels  8.71 us (9%)
  other arithmetic  6.57 us (7%)
  local copies, waits for them, and re-layouts  6.18 us (6%)
  between operations  5.18 us (5%)
    ppermute x12, starting transfers between devices, swap(): lax.ppermute(values, axis, [(i, i ^ flip) for i in range(lax.axis_size(ax...  28.7 us
    ppermute x12, waiting for transfers between devices, swap(): lax.ppermute(values, axis, [(i, i ^ flip) for i in range(lax.axis_size(ax...  26.5 us
    pallas_call x1, Pallas kernels, local_block(): pl.pallas_call(block_kernel, out_shape=(jax.ShapeDtypeStruct(feats_own.sh...  8.71 us
    ppermute x2, starting transfers between devices, extended(): lax.ppermute(head, axis, [((i + 1) % count, i) for i in range(ends)])  6.9 us
    ppermute x2, starting transfers between devices, extended(): lax.ppermute(tail, axis, [(i, (i + 1) % count) for i in range(ends)])  6.59 us
    unnamed x13, local copies, waits for them, and re-layouts  2.09 us
    ppermute x2, waiting for transfers between devices, extended(): lax.ppermute(tail, axis, [(i, (i + 1) % count) for i in range(ends)])  1.99 us
  transfers between devices with their start and end apart: 16, of which 11 were waited for; matrix products, arithmetic and copies ran while one was open for 2% of the time, Pallas kernels for 0%

profile of v1, /device:TPU:1, one launch (start us, length us, event | category | flops | bytes accessed | tf_op | source)
XLA Modules:
  0.0 97.3 jit_solution(12036878315040978380)
XLA Ops:
  0.6 0.0 copy-start
  0.7 1.1 %fusion.1 = (bf16[8,2,32,96]{3,2,1,0:T(8,128)(2,1)S(1)}, bf16[8,2,32,96]{3,2,1,0:T(8,128)(2,1)S(1)}) fusion(bf16[4,4,32,96]{3,2,1,0:T(8,128)(2,1)} %bitcast.46, bf16[4,4,32,96]{3,2,1,0:T(8,128)(2,1)} %bitcast.50), kind=kLoop, calls=%fused_computation.13 | loop fusion | flops 98304 | bytes 393216 | tf_op jit(solution)/shard_map/concatenate | solution.py:241
  1.7 1.3 %collective-permute-start.1 = (bf16[8,2,32,96]{3,2,1,0:T(8,128)(2,1)S(1)}, bf16[8,2,32,96]{3,2,1,0:T(8,128)(2,1)S(1)}, u32[]{:S(2)}, u32[]{:S(2)}) collective-permute-start(bf16[8,2,32,96]{3,2,1,0:T(8,128)(2,1)S(1)} %get-tuple-element.15), channel_id=1, source_target_pairs={{16,0},{32,16},{48,32},{64,48},{80,64},{96,80},{112,96},{128,112},... | collective-permute-start | bytes 294920 | tf_op jit(solution)/shard_map/ppermute | solution.py:206
  3.0 4.7 %collective-permute-start = (bf16[8,2,32,96]{3,2,1,0:T(8,128)(2,1)S(1)}, bf16[8,2,32,96]{3,2,1,0:T(8,128)(2,1)S(1)}, u32[]{:S(2)}, u32[]{:S(2)}) collective-permute-start(bf16[8,2,32,96]{3,2,1,0:T(8,128)(2,1)S(1)} %get-tuple-element.14), channel_id=1, source_target_pairs={{0,16},{16,32},{32,48},{48,64},{64,80},{80,96},{96,112},{112,128},... | collective-permute-start | bytes 294920 | tf_op jit(solution)/shard_map/ppermute | solution.py:204
  7.8 0.2 fusion.8.perm
  8.0 0.7 select_maximum_fusion.vectors
  8.7 0.9 collective-permute-done
  9.6 0.9 pad_maximum_fusion.6
  10.5 5.6 %collective-permute-start.3 = (bf16[8,8,2,96]{3,2,1,0:T(2,128)(2,1)S(1)}, bf16[8,8,2,96]{3,2,1,0:T(2,128)(2,1)S(1)}, u32[]{:S(2)}, u32[]{:S(2)}) collective-permute-start(bf16[8,8,2,96]{3,2,1,0:T(2,128)(2,1)S(1)} %get-tuple-element.10), channel_id=1, source_target_pairs={{2,0},{4,2},{6,4},{8,6},{10,8},{12,10},{14,12},{3,1},{5,3},{7,5},{... | collective-permute-start | bytes 73736 | tf_op jit(solution)/shard_map/ppermute | solution.py:206
  16.1 1.9 %collective-permute-start.2 = (bf16[8,8,2,96]{3,2,1,0:T(2,128)(2,1)S(1)}, bf16[8,8,2,96]{3,2,1,0:T(2,128)(2,1)S(1)}, u32[]{:S(2)}, u32[]{:S(2)}) collective-permute-start(bf16[8,8,2,96]{3,2,1,0:T(2,128)(2,1)S(1)} %get-tuple-element.9), channel_id=1, source_target_pairs={{0,2},{2,4},{4,6},{6,8},{8,10},{10,12},{12,14},{1,3},{3,5},{5,7},{... | collective-permute-start | bytes 73736 | tf_op jit(solution)/shard_map/ppermute | solution.py:204
  18.1 0.1 pad_add_fusion.edge
  18.2 1.1 %collective-permute-done.2 = bf16[8,8,2,96]{3,2,1,0:T(2,128)(2,1)S(1)} collective-permute-done((bf16[8,8,2,96]{3,2,1,0:T(2,128)(2,1)S(1)}, bf16[8,8,2,96]{3,2,1,0:T(2,128)(2,1)S(1)}, u32[]{:S(2)}, u32[]{:S(2)}) %collective-permute-start.2) | collective-permute-done | bytes 24608 | tf_op jit(solution)/shard_map/ppermute | solution.py:204
  19.2 0.3 pad_maximum_fusion.ext
  19.6 0.0 copy-start.3
  19.6 1.1 %copy-done.3 = bf16[3,3,3,96,96]{4,3,2,1,0:T(8,128)(2,1)S(1)} copy-done((bf16[3,3,3,96,96]{4,3,2,1,0:T(8,128)(2,1)S(1)}, bf16[3,3,3,96,96]{4,3,2,1,0:T(8,128)(2,1)}, u32[]{:S(2)}) %copy-start.3) | copy-done | bytes 497688
  20.7 8.7 %shard_map.104 = (f32[4,4,32,96]{3,2,1,0:T(8,128)S(1)}, f32[2,4,168,384]{3,2,1,0:T(8,128)S(1)}) custom-call(s32[4]{0:T(128)S(1)} %pad_add_fusion.edge, bf16[8,8,36,96]{3,2,1,0:T(8,128)(2,1)S(1)} %pad_maximum_fusion.ext, bf16[4,4,32,96]{3,2,1,0:T(8,128)(2,1)S(1)} %bitcast.49, bf16[4,4,32,96]{3,2,1,0:T(8,128)(2,1)S(1)} %bitcast.53, ...), custom_call_target="tpu_custom_call" | custom-call | flops 3000000000 | bytes 6000000 | tf_op jit(solution)/shard_map/pallas_call | solution.py:173
  29.4 1.0 %dynamic-slice_bitcast_fusion = f32[4,168,384]{2,1,0:T(8,128)} fusion(f32[2,4,168,384]{3,2,1,0:T(8,128)S(1)} %get-tuple-element.5, s32[]{:T(128)S(6)} %select_n.116), kind=kLoop, calls=%fused_computation.1 | loop fusion | bytes 2064388 | tf_op jit(solution)/shard_map/jit(dynamic_index_in_dim)/squeeze | solution.py:217
  30.4 0.2 collective-permute-start.4
  30.6 2.8 %collective-permute-done.4 = f32[4,168,384]{2,1,0:T(8,128)} collective-permute-done((f32[4,168,384]{2,1,0:T(8,128)}, f32[4,168,384]{2,1,0:T(8,128)}, u32[]{:S(2)}, u32[]{:S(2)}) %collective-permute-start.4) | collective-permute-done | bytes 1032224 | tf_op jit(solution)/shard_map/ppermute | solution.py:213
  33.4 1.4 %bitcast_add_fusion = f32[4,168,384]{2,1,0:T(8,128)S(1)} fusion(f32[4,168,384]{2,1,0:T(8,128)} %collective-permute-done.4, f32[2,4,168,384]{3,2,1,0:T(8,128)S(1)} %get-tuple-element.5, s32[]{:T(128)S(6)} %select_n.115), kind=kLoop, calls=%fused_computation | loop fusion | flops 258048 | bytes 3096580 | tf_op jit(solution)/shard_map/add | solution.py:268
  34.8 1.0 copy-done.4
  35.7 0.1 dynamic-slice_bitcast_fusion.1
  35.8 2.3 %collective-permute-start.5 = (f32[168,384]{1,0:T(8,128)S(1)}, f32[168,384]{1,0:T(8,128)S(1)}, u32[]{:S(2)}, u32[]{:S(2)}) collective-permute-start(f32[168,384]{1,0:T(8,128)S(1)} %get-tuple-element.8), channel_id=1, source_target_pairs={{0,16},{16,0},{32,48},{48,32},{64,80},{80,64},{96,112},{112,96},{1... | collective-permute-start | bytes 774152 | tf_op jit(solution)/shard_map/ppermute | solution.py:213
  38.1 5.3 %collective-permute-start.6 = (f32[168,384]{1,0:T(8,128)S(1)}, f32[168,384]{1,0:T(8,128)S(1)}, u32[]{:S(2)}, u32[]{:S(2)}) collective-permute-start(f32[168,384]{1,0:T(8,128)S(1)} %get-tuple-element.7), channel_id=1, source_target_pairs={{0,32},{16,48},{32,0},{48,16},{64,96},{80,112},{96,64},{112,80},{1... | collective-permute-start | bytes 774152 | tf_op jit(solution)/shard_map/ppermute | solution.py:213
  43.4 1.1 %collective-permute-done.5 = f32[168,384]{1,0:T(8,128)S(1)} collective-permute-done((f32[168,384]{1,0:T(8,128)S(1)}, f32[168,384]{1,0:T(8,128)S(1)}, u32[]{:S(2)}, u32[]{:S(2)}) %collective-permute-start.5) | collective-permute-done | bytes 258080 | tf_op jit(solution)/shard_map/ppermute | solution.py:213
  44.5 10.7 %collective-permute-done.6 = f32[168,384]{1,0:T(8,128)S(1)} collective-permute-done((f32[168,384]{1,0:T(8,128)S(1)}, f32[168,384]{1,0:T(8,128)S(1)}, u32[]{:S(2)}, u32[]{:S(2)}) %collective-permute-start.6) | collective-permute-done | bytes 258080 | tf_op jit(solution)/shard_map/ppermute | solution.py:213
  55.2 2.0 %collective-permute-done.7 = f32[168,384]{1,0:T(8,128)S(1)} collective-permute-done((f32[168,384]{1,0:T(8,128)S(1)}, f32[168,384]{1,0:T(8,128)S(1)}, u32[]{:S(2)}, u32[]{:S(2)}) %collective-permute-start.7) | collective-permute-done | bytes 258080 | tf_op jit(solution)/shard_map/ppermute | solution.py:213
  57.2 1.0 %fusion = f32[168,384]{1,0:T(8,128)S(1)} fusion(f32[168,384]{1,0:T(8,128)S(1)} %collective-permute-done.5, f32[168,384]{1,0:T(8,128)S(1)} %collective-permute-done.6, f32[168,384]{1,0:T(8,128)S(1)} %collective-permute-done.7, f32[4,168,384]{2,1,0:T(8,128)} %copy-done.4, s32[]{:T(128)S(6)} %select_n.118), kind=kLoop, calls=%fused_computation.7 | loop fusion | flops 193536 | bytes 1290244 | tf_op jit(solution)/shard_map/add | solution.py:270
  58.3 5.8 %collective-permute-start.8 = (f32[42,384]{1,0:T(8,128)S(1)}, f32[42,384]{1,0:T(8,128)S(1)}, u32[]{:S(2)}, u32[]{:S(2)}) collective-permute-start(f32[42,384]{1,0:T(8,128)S(1)} %get-tuple-element.13), channel_id=1, source_target_pairs={{0,64},{16,80},{32,96},{48,112},{64,0},{80,16},{96,32},{112,48},{1... | collective-permute-start | bytes 193544 | tf_op jit(solution)/shard_map/ppermute | solution.py:213
  64.1 5.9 %collective-permute-start.9 = (f32[42,384]{1,0:T(8,128)S(1)}, f32[42,384]{1,0:T(8,128)S(1)}, u32[]{:S(2)}, u32[]{:S(2)}) collective-permute-start(f32[42,384]{1,0:T(8,128)S(1)} %get-tuple-element.12), channel_id=1, source_target_pairs={{0,128},{16,144},{32,160},{48,176},{64,192},{80,208},{96,224},{112... | collective-permute-start | bytes 193544 | tf_op jit(solution)/shard_map/ppermute | solution.py:213
  70.0 3.9 %collective-permute-done.9 = f32[42,384]{1,0:T(8,128)S(1)} collective-permute-done((f32[42,384]{1,0:T(8,128)S(1)}, f32[42,384]{1,0:T(8,128)S(1)}, u32[]{:S(2)}, u32[]{:S(2)}) %collective-permute-start.9) | collective-permute-done | bytes 64544 | tf_op jit(solution)/shard_map/ppermute | solution.py:213
  73.9 1.8 %collective-permute-done.10 = f32[42,384]{1,0:T(8,128)S(1)} collective-permute-done((f32[42,384]{1,0:T(8,128)S(1)}, f32[42,384]{1,0:T(8,128)S(1)}, u32[]{:S(2)}, u32[]{:S(2)}) %collective-permute-start.10) | collective-permute-done | bytes 64544 | tf_op jit(solution)/shard_map/ppermute | solution.py:213
  75.7 4.0 %collective-permute-start.12 = (f32[42,384]{1,0:T(8,128)S(1)}, f32[42,384]{1,0:T(8,128)S(1)}, u32[]{:S(2)}, u32[]{:S(2)}) collective-permute-start(f32[42,384]{1,0:T(8,128)S(1)} %fusion.2), channel_id=1, source_target_pairs={{0,8},{2,10},{4,12},{6,14},{8,0},{10,2},{12,4},{14,6},{1,9},{3,11}... | collective-permute-start | bytes 193544 | tf_op jit(solution)/shard_map/ppermute | solution.py:213
  79.7 0.4 collective-permute-start.13
  80.1 1.3 %collective-permute-done.12 = f32[42,384]{1,0:T(8,128)S(1)} collective-permute-done((f32[42,384]{1,0:T(8,128)S(1)}, f32[42,384]{1,0:T(8,128)S(1)}, u32[]{:S(2)}, u32[]{:S(2)}) %collective-permute-start.12) | collective-permute-done | bytes 64544 | tf_op jit(solution)/shard_map/ppermute | solution.py:213
  81.4 2.7 %collective-permute-done.13 = f32[42,384]{1,0:T(8,128)S(1)} collective-permute-done((f32[42,384]{1,0:T(8,128)S(1)}, f32[42,384]{1,0:T(8,128)S(1)}, u32[]{:S(2)}, u32[]{:S(2)}) %collective-permute-start.13) | collective-permute-done | bytes 64544 | tf_op jit(solution)/shard_map/ppermute | solution.py:213
  84.1 0.1 collective-permute-start.14
  84.2 0.6 fusion.9
  87.6 0.6 slice.48
  88.2 0.6 slice.49
  90.3 4.7 %collective-permute-start.15 = (f32[42,384]{1,0:T(8,128)S(1)}, f32[42,384]{1,0:T(8,128)S(1)}, u32[]{:S(2)}, u32[]{:S(2)}) collective-permute-start(f32[42,384]{1,0:T(8,128)S(1)} %add_multiply_fusion), channel_id=1, source_target_pairs={{0,2},{2,0},{4,6},{6,4},{8,10},{10,8},{12,14},{14,12},{1,3},{3,1},... | collective-permute-start | bytes 193544 | tf_op jit(solution)/shard_map/ppermute | solution.py:213
  95.0 0.7 multiply_bitcast_fusion
  95.7 0.2 collective-permute-done.15
  96.1 0.1 slice.51
  96.3 0.2 reshape.58
  96.4 0.1 pad_maximum_fusion.1
  96.5 0.1 copy.16
  96.6 0.7 slice.52
  (33 shorter events, 0.4 us)
Async XLA Ops:
  0.6 18.6 %copy-start = (bf16[1,4,4,32,96]{4,3,2,1,0:T(8,128)(2,1)S(1)}, bf16[1,4,4,32,96]{4,3,2,1,0:T(8,128)(2,1)}, u32[]{:S(2)}) copy-start(bf16[1,4,4,32,96]{4,3,2,1,0:T(8,128)(2,1)} %param.9) | copy-start | bytes 294916
  0.6 18.6 %copy-start.1 = (bf16[1,4,4,32,96]{4,3,2,1,0:T(8,128)(2,1)S(1)}, bf16[1,4,4,32,96]{4,3,2,1,0:T(8,128)(2,1)}, u32[]{:S(2)}) copy-start(bf16[1,4,4,32,96]{4,3,2,1,0:T(8,128)(2,1)} %param.16) | copy-start | bytes 294916
  0.7 18.9 %copy-start.2 = (bf16[3,3,3,96,96]{4,3,2,1,0:T(8,128)(2,1)S(1)}, bf16[3,3,3,96,96]{4,3,2,1,0:T(8,128)(2,1)}, u32[]{:S(2)}) copy-start(bf16[3,3,3,96,96]{4,3,2,1,0:T(8,128)(2,1)} %param.12) | copy-start | bytes 1492996
  1.7 7.0 %collective-permute-start.1 = (bf16[8,2,32,96]{3,2,1,0:T(8,128)(2,1)S(1)}, bf16[8,2,32,96]{3,2,1,0:T(8,128)(2,1)S(1)}, u32[]{:S(2)}, u32[]{:S(2)}) collective-permute-start(bf16[8,2,32,96]{3,2,1,0:T(8,128)(2,1)S(1)} %get-tuple-element.15), channel_id=1, source_target_pairs={{16,0},{32,16},{48,32},{64,48},{80,64},{96,80},{112,96},{128,112},... | collective-permute-start | bytes 294920 | tf_op jit(solution)/shard_map/ppermute | solution.py:206
  3.0 6.6 %collective-permute-start = (bf16[8,2,32,96]{3,2,1,0:T(8,128)(2,1)S(1)}, bf16[8,2,32,96]{3,2,1,0:T(8,128)(2,1)S(1)}, u32[]{:S(2)}, u32[]{:S(2)}) collective-permute-start(bf16[8,2,32,96]{3,2,1,0:T(8,128)(2,1)S(1)} %get-tuple-element.14), channel_id=1, source_target_pairs={{0,16},{16,32},{32,48},{48,64},{64,80},{80,96},{96,112},{112,128},... | collective-permute-start | bytes 294920 | tf_op jit(solution)/shard_map/ppermute | solution.py:204
  10.5 7.6 %collective-permute-start.3 = (bf16[8,8,2,96]{3,2,1,0:T(2,128)(2,1)S(1)}, bf16[8,8,2,96]{3,2,1,0:T(2,128)(2,1)S(1)}, u32[]{:S(2)}, u32[]{:S(2)}) collective-permute-start(bf16[8,8,2,96]{3,2,1,0:T(2,128)(2,1)S(1)} %get-tuple-element.10), channel_id=1, source_target_pairs={{2,0},{4,2},{6,4},{8,6},{10,8},{12,10},{14,12},{3,1},{5,3},{7,5},{... | collective-permute-start | bytes 73736 | tf_op jit(solution)/shard_map/ppermute | solution.py:206
  16.1 3.1 %collective-permute-start.2 = (bf16[8,8,2,96]{3,2,1,0:T(2,128)(2,1)S(1)}, bf16[8,8,2,96]{3,2,1,0:T(2,128)(2,1)S(1)}, u32[]{:S(2)}, u32[]{:S(2)}) collective-permute-start(bf16[8,8,2,96]{3,2,1,0:T(2,128)(2,1)S(1)} %get-tuple-element.9), channel_id=1, source_target_pairs={{0,2},{2,4},{4,6},{6,8},{8,10},{10,12},{12,14},{1,3},{3,5},{5,7},{... | collective-permute-start | bytes 73736 | tf_op jit(solution)/shard_map/ppermute | solution.py:204
  19.6 1.1 %copy-start.3 = (bf16[3,3,3,96,96]{4,3,2,1,0:T(8,128)(2,1)S(1)}, bf16[3,3,3,96,96]{4,3,2,1,0:T(8,128)(2,1)}, u32[]{:S(2)}) copy-start(bf16[3,3,3,96,96]{4,3,2,1,0:T(8,128)(2,1)} %param.15) | copy-start | bytes 1492996
  30.4 3.0 %collective-permute-start.4 = (f32[4,168,384]{2,1,0:T(8,128)}, f32[4,168,384]{2,1,0:T(8,128)}, u32[]{:S(2)}, u32[]{:S(2)}) collective-permute-start(f32[4,168,384]{2,1,0:T(8,128)} %dynamic-slice_bitcast_fusion), channel_id=1, source_target_pairs={{0,2},{2,0},{4,6},{6,4},{8,10},{10,8},{12,14},{14,12},{1,3},{3,1},... | collective-permute-start | bytes 3096584 | tf_op jit(solution)/shard_map/ppermute | solution.py:213
  34.8 1.0 %copy-start.4 = (f32[4,168,384]{2,1,0:T(8,128)}, f32[4,168,384]{2,1,0:T(8,128)S(1)}, u32[]{:S(2)}) copy-start(f32[4,168,384]{2,1,0:T(8,128)S(1)} %bitcast_add_fusion) | copy-start | bytes 3096580
  35.8 8.7 %collective-permute-start.5 = (f32[168,384]{1,0:T(8,128)S(1)}, f32[168,384]{1,0:T(8,128)S(1)}, u32[]{:S(2)}, u32[]{:S(2)}) collective-permute-start(f32[168,384]{1,0:T(8,128)S(1)} %get-tuple-element.8), channel_id=1, source_target_pairs={{0,16},{16,0},{32,48},{48,32},{64,80},{80,64},{96,112},{112,96},{1... | collective-permute-start | bytes 774152 | tf_op jit(solution)/shard_map/ppermute | solution.py:213
  38.1 17.1 %collective-permute-start.6 = (f32[168,384]{1,0:T(8,128)S(1)}, f32[168,384]{1,0:T(8,128)S(1)}, u32[]{:S(2)}, u32[]{:S(2)}) collective-permute-start(f32[168,384]{1,0:T(8,128)S(1)} %get-tuple-element.7), channel_id=1, source_target_pairs={{0,32},{16,48},{32,0},{48,16},{64,96},{80,112},{96,64},{112,80},{1... | collective-permute-start | bytes 774152 | tf_op jit(solution)/shard_map/ppermute | solution.py:213
  43.4 13.8 %collective-permute-start.7 = (f32[168,384]{1,0:T(8,128)S(1)}, f32[168,384]{1,0:T(8,128)S(1)}, u32[]{:S(2)}, u32[]{:S(2)}) collective-permute-start(f32[168,384]{1,0:T(8,128)S(1)} %get-tuple-element.6), channel_id=1, source_target_pairs={{0,48},{16,32},{32,16},{48,0},{64,112},{80,96},{96,80},{112,64},{1... | collective-permute-start | bytes 774152 | tf_op jit(solution)/shard_map/ppermute | solution.py:213
  43.4 40.8 %copy-start.5 = (f32[2]{0:T(128)S(1)}, f32[2]{0:T(128)}, u32[]{:S(2)}) copy-start(f32[2]{0:T(128)} %param.17) | copy-start | bytes 28
  58.3 11.7 %collective-permute-start.8 = (f32[42,384]{1,0:T(8,128)S(1)}, f32[42,384]{1,0:T(8,128)S(1)}, u32[]{:S(2)}, u32[]{:S(2)}) collective-permute-start(f32[42,384]{1,0:T(8,128)S(1)} %get-tuple-element.13), channel_id=1, source_target_pairs={{0,64},{16,80},{32,96},{48,112},{64,0},{80,16},{96,32},{112,48},{1... | collective-permute-start | bytes 193544 | tf_op jit(solution)/shard_map/ppermute | solution.py:213
  64.1 9.8 %collective-permute-start.9 = (f32[42,384]{1,0:T(8,128)S(1)}, f32[42,384]{1,0:T(8,128)S(1)}, u32[]{:S(2)}, u32[]{:S(2)}) collective-permute-start(f32[42,384]{1,0:T(8,128)S(1)} %get-tuple-element.12), channel_id=1, source_target_pairs={{0,128},{16,144},{32,160},{48,176},{64,192},{80,208},{96,224},{112... | collective-permute-start | bytes 193544 | tf_op jit(solution)/shard_map/ppermute | solution.py:213
  70.0 5.7 %collective-permute-start.10 = (f32[42,384]{1,0:T(8,128)S(1)}, f32[42,384]{1,0:T(8,128)S(1)}, u32[]{:S(2)}, u32[]{:S(2)}) collective-permute-start(f32[42,384]{1,0:T(8,128)S(1)} %get-tuple-element.11), channel_id=1, source_target_pairs={{0,192},{16,208},{32,224},{48,240},{64,128},{80,144},{96,160},{112... | collective-permute-start | bytes 193544 | tf_op jit(solution)/shard_map/ppermute | solution.py:213
  75.7 5.7 %collective-permute-start.12 = (f32[42,384]{1,0:T(8,128)S(1)}, f32[42,384]{1,0:T(8,128)S(1)}, u32[]{:S(2)}, u32[]{:S(2)}) collective-permute-start(f32[42,384]{1,0:T(8,128)S(1)} %fusion.2), channel_id=1, source_target_pairs={{0,8},{2,10},{4,12},{6,14},{8,0},{10,2},{12,4},{14,6},{1,9},{3,11}... | collective-permute-start | bytes 193544 | tf_op jit(solution)/shard_map/ppermute | solution.py:213
  79.7 4.4 %collective-permute-start.13 = (f32[42,384]{1,0:T(8,128)S(1)}, f32[42,384]{1,0:T(8,128)S(1)}, u32[]{:S(2)}, u32[]{:S(2)}) collective-permute-start(f32[42,384]{1,0:T(8,128)S(1)} %fusion.2), channel_id=1, source_target_pairs={{0,12},{2,14},{4,8},{6,10},{8,4},{10,6},{12,0},{14,2},{1,13},{3,15... | collective-permute-start | bytes 193544 | tf_op jit(solution)/shard_map/ppermute | solution.py:213
  80.1 4.0 %collective-permute-start.11 = (f32[42,384]{1,0:T(8,128)S(1)}, f32[42,384]{1,0:T(8,128)S(1)}, u32[]{:S(2)}, u32[]{:S(2)}) collective-permute-start(f32[42,384]{1,0:T(8,128)S(1)} %fusion.2), channel_id=1, source_target_pairs={{0,4},{2,6},{4,0},{6,2},{8,12},{10,14},{12,8},{14,10},{1,5},{3,7},... | collective-permute-start | bytes 193544 | tf_op jit(solution)/shard_map/ppermute | solution.py:213
  84.1 3.5 %collective-permute-start.14 = (f32[42,384]{1,0:T(8,128)S(1)}, f32[42,384]{1,0:T(8,128)S(1)}, u32[]{:S(2)}, u32[]{:S(2)}) collective-permute-start(f32[42,384]{1,0:T(8,128)S(1)} %add_add_fusion), channel_id=1, source_target_pairs={{0,1},{1,0},{2,3},{3,2},{4,5},{5,4},{6,7},{7,6},{8,9},{9,8},{10,11... | collective-permute-start | bytes 193544 | tf_op jit(solution)/shard_map/ppermute | solution.py:213
  90.3 5.6 %collective-permute-start.15 = (f32[42,384]{1,0:T(8,128)S(1)}, f32[42,384]{1,0:T(8,128)S(1)}, u32[]{:S(2)}, u32[]{:S(2)}) collective-permute-start(f32[42,384]{1,0:T(8,128)S(1)} %add_multiply_fusion), channel_id=1, source_target_pairs={{0,2},{2,0},{4,6},{6,4},{8,10},{10,8},{12,14},{14,12},{1,3},{3,1},... | collective-permute-start | bytes 193544 | tf_op jit(solution)/shard_map/ppermute | solution.py:213
